TPU v7x, 256 devices: a whole 4x4x8 slice. The times are simulated.
256 devices in a mesh: rep: 32 (over z, y_lo, core), fsdp: 8 (over y_hi, x).
Axes of the slice: x: 4, y: 4 (y_hi: 2, y_lo: 2; y = y_hi * 2 + y_lo), z: 8, core: 2. Of those that a mesh axis runs over, the one named last changes fastest.
Arguments:
- tokens: bfloat16 [32768, 1536], P(('rep', 'fsdp')), may hold values from -6 to 6
- segment_ids: int32 [32768], P('rep'), may hold values from 0 to 3, as said below
- routes: int32 [32768, 6], P(('rep', 'fsdp')), may hold values from 0 to 7, all different within a row
- gain_attn: bfloat16 [1536], P('fsdp'), may hold values from 0.099609375 to 1.8984375
- w_query: bfloat16 [1536, 1536], P('fsdp'), may hold values from -0.3125 to 0.3125
- w_key: bfloat16 [1536, 512], P('fsdp'), may hold values from -0.15625 to 0.15625
- w_value: bfloat16 [1536, 512], P('fsdp'), may hold values from -0.15625 to 0.15625
- w_out: bfloat16 [1536, 1536], P('fsdp'), may hold values from -0.625 to 0.625
- gain_ffn: bfloat16 [1536], P('fsdp'), may hold values from 0.099609375 to 1.8984375
- w_router: bfloat16 [1536, 8], P('fsdp'), may hold values from -0.078125 to 0.078125
- w_shared_in: bfloat16 [1536, 2048], P('fsdp'), may hold values from -0.15625 to 0.15625
- w_shared_out: bfloat16 [1024, 1536], P('fsdp'), may hold values from -0.375 to 0.375
- w_expert_in: bfloat16 [1536, 8, 1024], P('fsdp'), may hold values from -0.15625 to 0.15625
- w_expert_out: bfloat16 [8, 512, 1536], P(None, 'fsdp'), may hold values from -1 to 1
- cotangent: bfloat16 [32768, 1536], P(('rep', 'fsdp')), may hold values from -6 to 6
Outputs:
- result: bfloat16 [32768, 1536], P(('rep', 'fsdp'))
- grad_input: bfloat16 [32768, 1536], P(('rep', 'fsdp'))
- grad_gain_attn: float32 [1536], P('fsdp')
- grad_query: float32 [1536, 1536], P('fsdp')
- grad_key: float32 [1536, 512], P('fsdp')
- grad_value: float32 [1536, 512], P('fsdp')
- grad_out: float32 [1536, 1536], P('fsdp')
- grad_gain_ffn: float32 [1536], P('fsdp')
- grad_router: float32 [1536, 8], P('fsdp')
- grad_shared_in: float32 [1536, 2048], P('fsdp')
- grad_shared_out: float32 [1024, 1536], P('fsdp')
- grad_expert_in: float32 [1536, 8, 1024], P('fsdp')
- grad_expert_out: float32 [8, 512, 1536], P(None, 'fsdp')
Inputs may be any that keep to these rules, and one draw needn't show every extreme that they name: `segment_ids`: within each sequence of 1024 tokens, documents 1, 2, 3 follow one another and padding 0 closes the sequence; document 2 begins on the sequence's first device and ends on its last. `routes`: 6 different experts for each token.
All inputs are finite; a program needn't handle non-finite values.
Results may differ from a plain program's by a relative error of at most 0.03.
Values may be sent and summed in bfloat16 or wider, within the bound.
No kernel may reach another device: no remote copies, remote signals or barrier semaphores. Data moves between devices by JAX's collectives and lax.ppermute only.
A program may use at most 256 MiB of HBM per device.

v0:
```python
import math
import jax
import jax.numpy as jnp
from jax import lax
from jax.sharding import PartitionSpec as P

HEADS = 12
KV_HEADS = 4
HEAD = 128
FE = 512
FS = 1024
eps_norm = 1e-05


def side_by_side(arrays, axis, dim, along):
    widths = [math.prod(a.shape[along:]) for a in arrays]
    both = jnp.concatenate(
        [a.reshape(*a.shape[:along], w) for a, w in zip(arrays, widths)], axis=along
    )
    whole = lax.all_gather(both, axis, axis=dim, tiled=True)
    pieces = jnp.split(whole, [sum(widths[:k]) for k in range(1, len(widths))], axis=along)
    return tuple(
        (b.reshape(*whole.shape[:along], *a.shape[along:]) for a, b in zip(arrays, pieces))
    )


def side_by_side_2(arrays, axis, dim, along):
    ends, at = ([], 0)
    for a in arrays[:-1]:
        at += a.shape[along]
        ends.append(at)
    both = jnp.concatenate(arrays, axis=along)
    return tuple(jnp.split(lax.all_gather(both, axis, axis=dim, tiled=True), ends, axis=along))


def joined_along(pieces, dim):
    lengths = list(pieces.shape[1:])
    lengths[dim] *= pieces.shape[0]
    return jnp.moveaxis(pieces, 0, dim).reshape(lengths)


def gather_packed(arrays, axis, dims):
    flat = jnp.concatenate([a.reshape(-1) for a in arrays])
    lines, at, gathered = (lax.all_gather(flat, axis), 0, [])
    for a, dim in zip(arrays, dims):
        pieces = lines[:, at : at + a.size].reshape(-1, *a.shape)
        gathered.append(joined_along(pieces, dim))
        at += a.size
    return tuple(gathered)


def in_blocks(array, dim, length):
    before, after = (array.shape[:dim], array.shape[dim + 1 :])
    return jnp.moveaxis(array.reshape(*before, length, -1, *after), dim, 0)


def summed_on_arrival(array, axis, dim):
    length = lax.axis_size(axis)
    pieces = lax.all_to_all(in_blocks(array, dim, length), axis, 0, 0, tiled=True)
    return jnp.sum(pieces, axis=0)


def in_one_piece(arrays, axis, dim, along):
    widths = [a.shape[along] for a in arrays]
    both = jnp.concatenate(arrays, axis=along)
    whole = lax.psum_scatter(both, axis, scatter_dimension=dim, tiled=True)
    return tuple(jnp.split(whole, [sum(widths[:k]) for k in range(1, len(widths))], axis=along))


def sent_together(arrays, axis, dim, along):
    columns = [a.reshape(*a.shape[:along], -1) for a in arrays]
    both = jnp.concatenate(columns, axis=along)
    whole, at, gathered = (lax.psum_scatter(both, axis, scatter_dimension=dim, tiled=True), 0, [])
    for a, column in zip(arrays, columns):
        section = whole[..., at : at + column.shape[along]]
        gathered.append(section.reshape(*section.shape[:along], *a.shape[along:]))
        at += column.shape[along]
    return tuple(gathered)


def dot_rows(left, right):
    return lax.dot_general(
        left, right, (((1,), (1,)), ((), ())), preferred_element_type=jnp.float32
    )


def dot_cols(left, right):
    return lax.dot_general(
        left, right, (((0,), (0,)), ((), ())), preferred_element_type=jnp.float32
    )


def normalize(values):
    factor = lax.rsqrt(jnp.mean(values * values, axis=-1, keepdims=True) + eps_norm)
    return (values * factor, factor)


def norm_back(grad_normed, unit, factor, gain):
    scaled = grad_normed * gain
    gain_grad = jnp.sum(grad_normed * unit, axis=0)
    inner = jnp.mean(scaled * unit, axis=-1, keepdims=True)
    return (factor * (scaled - unit * inner), gain_grad)


def silu_slope(values, sig):
    return sig * (1.0 + values * (1.0 - sig))


def shards(
    tokens,
    segment_ids,
    routes,
    gain_attn,
    w_query,
    w_key,
    w_value,
    w_out,
    gain_ffn,
    w_router,
    w_shared_in,
    w_shared_out,
    w_expert_in,
    w_expert_out,
    cotangent,
):
    local_rows = tokens.shape[0]
    group_len = segment_ids.shape[0]
    per_group = HEADS // KV_HEADS
    qk_scale = 1.0 / math.sqrt(HEAD)
    experts_count = w_router.shape[1]
    start_row = lax.axis_index("fsdp") * local_rows
    seg_local = lax.dynamic_slice_in_dim(segment_ids, start_row, local_rows)
    query_pos = start_row + jnp.arange(local_rows, dtype=jnp.int32)
    key_pos = jnp.arange(group_len, dtype=jnp.int32)
    allowed = (query_pos[:, None] == key_pos[None, :]) | (key_pos[None, :] < query_pos[:, None]) & (
        seg_local[:, None] == segment_ids[None, :]
    ) & (segment_ids[None, :] != 0)
    inputs = tokens.astype(jnp.float32)
    attn_in = side_by_side((gain_attn, w_query, w_key, w_value), "fsdp", 0, 1)
    unit_one, factor_one = normalize(inputs)
    gain_one = attn_in[0].astype(jnp.float32)
    normed_one = (unit_one * gain_one).astype(jnp.bfloat16)
    query = jnp.dot(normed_one, attn_in[1], preferred_element_type=jnp.float32).astype(jnp.bfloat16)
    key_local = jnp.dot(normed_one, attn_in[2], preferred_element_type=jnp.float32).astype(
        jnp.bfloat16
    )
    value_local = jnp.dot(normed_one, attn_in[3], preferred_element_type=jnp.float32).astype(
        jnp.bfloat16
    )
    keys_all, values_all = side_by_side_2((key_local, value_local), "fsdp", 0, 1)
    query_heads = query.reshape(local_rows, KV_HEADS, per_group, HEAD)
    key_heads = keys_all.reshape(group_len, KV_HEADS, HEAD)
    value_heads = values_all.reshape(group_len, KV_HEADS, HEAD)

    def scores_of():
        raw = (
            jnp.einsum("tkgd,skd->kgts", query_heads, key_heads, preferred_element_type=jnp.float32)
            * qk_scale
        )
        return jnp.where(allowed[None, None], raw, -1e30)

    scores = scores_of()
    top_score = jnp.max(scores, axis=-1, keepdims=True)
    expo = jnp.exp(scores - top_score)
    total = jnp.sum(expo, axis=-1, keepdims=True)
    log_total = top_score + jnp.log(total)
    probs = (expo / total).astype(jnp.bfloat16)
    attended = jnp.einsum("kgts,skd->tkgd", probs, value_heads, preferred_element_type=jnp.float32)
    attended = attended.reshape(local_rows, HEADS * HEAD).astype(jnp.bfloat16)
    out_full = lax.all_gather(w_out, "fsdp", axis=0, tiled=True)
    hidden = inputs + jnp.dot(attended, out_full, preferred_element_type=jnp.float32)
    ffn_in = (
        lax.all_gather(gain_ffn, "fsdp", axis=0, tiled=True),
        lax.all_gather(w_router, "fsdp", axis=0, tiled=True),
        lax.all_gather(w_shared_in, "fsdp", axis=0, tiled=True),
        lax.all_gather(w_expert_in, "fsdp", axis=0, tiled=True),
    )
    unit_two, factor_two = normalize(hidden)
    gain_two = ffn_in[0].astype(jnp.float32)
    normed_two = (unit_two * gain_two).astype(jnp.bfloat16)
    logits = jnp.dot(normed_two, ffn_in[1], preferred_element_type=jnp.float32)
    chosen = jnp.sum(
        (routes[:, :, None] == jnp.arange(experts_count, dtype=jnp.int32)[None, None, :]).astype(
            jnp.float32
        ),
        axis=1,
    )
    weighted = chosen * jnp.exp(logits)
    gates = weighted / jnp.sum(weighted, axis=-1, keepdims=True)
    expert_pre = jnp.einsum(
        "td,def->tef", normed_two, ffn_in[3], preferred_element_type=jnp.float32
    )
    gate_part = expert_pre[:, :, :FE]
    up_part = expert_pre[:, :, FE:]
    gate_sig = jax.nn.sigmoid(gate_part)
    activ = gate_part * gate_sig * up_part
    mixed = (gates[:, :, None] * activ).astype(jnp.bfloat16)
    shared_pre = jnp.dot(normed_two, ffn_in[2], preferred_element_type=jnp.float32)
    shared_gate = shared_pre[:, :FS]
    shared_up = shared_pre[:, FS:]
    shared_sig = jax.nn.sigmoid(shared_gate)
    shared_act = (shared_gate * shared_sig * shared_up).astype(jnp.bfloat16)
    ffn_out = gather_packed((w_expert_out, w_shared_out), "fsdp", (1, 0))
    result = hidden + jnp.einsum(
        "tef,efd->td", mixed, ffn_out[0], preferred_element_type=jnp.float32
    )
    result = result + jnp.dot(shared_act, ffn_out[1], preferred_element_type=jnp.float32)
    grad_top = cotangent.astype(jnp.float32)
    grad_mixed = jnp.einsum(
        "td,efd->tef", cotangent, ffn_out[0], preferred_element_type=jnp.float32
    )
    grad_shared = dot_rows(cotangent, ffn_out[1])
    grad_gates = jnp.sum(grad_mixed * activ, axis=-1)
    grad_activ = grad_mixed * gates[:, :, None]
    grad_pre = jnp.concatenate(
        [grad_activ * up_part * silu_slope(gate_part, gate_sig), grad_activ * gate_part * gate_sig],
        axis=-1,
    ).astype(jnp.bfloat16)
    grad_logits = (
        gates * (grad_gates - jnp.sum(gates * grad_gates, axis=-1, keepdims=True))
    ).astype(jnp.bfloat16)
    grad_spre = jnp.concatenate(
        [
            grad_shared * shared_up * silu_slope(shared_gate, shared_sig),
            grad_shared * shared_gate * shared_sig,
        ],
        axis=-1,
    ).astype(jnp.bfloat16)
    router_back, shared_back, expert_back = (ffn_in[1], ffn_in[2], ffn_in[3])
    grad_normed_two = jnp.einsum(
        "tef,def->td", grad_pre, expert_back, preferred_element_type=jnp.float32
    )
    grad_normed_two = (
        grad_normed_two + dot_rows(grad_spre, shared_back) + dot_rows(grad_logits, router_back)
    )
    grad_norm_two, grad_gain_ffn = norm_back(grad_normed_two, unit_two, factor_two, gain_two)
    grad_hidden = grad_top + grad_norm_two
    width_own = w_router.shape[0]
    col_start = lax.axis_index("fsdp") * width_own
    fe_own = w_expert_out.shape[1]
    fe_start = lax.axis_index("fsdp") * fe_own
    fs_own = w_shared_out.shape[0]
    fs_start = lax.axis_index("fsdp") * fs_own
    pieces = side_by_side((normed_two, grad_pre, grad_spre, grad_logits), "fsdp", 0, 1)
    part_normed = lax.dynamic_slice_in_dim(pieces[0], col_start, width_own, 1)
    router_part = dot_cols(part_normed, pieces[3])
    shared_part = dot_cols(part_normed, pieces[2])
    expert_part = jnp.einsum(
        "td,tef->def", part_normed, pieces[1], preferred_element_type=jnp.float32
    )
    shared_in_own = shared_part
    expert_in_own = expert_part
    pieces = side_by_side((mixed, shared_act, cotangent), "fsdp", 0, 1)
    part_mixed = lax.dynamic_slice_in_dim(pieces[0], fe_start, fe_own, 2)
    part_shared = lax.dynamic_slice_in_dim(pieces[1], fs_start, fs_own, 1)
    expert_part = jnp.einsum(
        "tef,td->efd", part_mixed, pieces[2], preferred_element_type=jnp.float32
    )
    shared_part = dot_cols(part_shared, pieces[2])
    gain_own = summed_on_arrival(grad_gain_ffn, "fsdp", 0)
    ffn_owned = (gain_own, router_part, shared_in_own, expert_in_own, shared_part, expert_part)
    hidden_low = grad_hidden.astype(jnp.bfloat16)
    grad_out = dot_cols(attended, hidden_low)
    grad_att = dot_rows(hidden_low, out_full).astype(jnp.bfloat16)
    grad_heads = grad_att.reshape(local_rows, KV_HEADS, per_group, HEAD)
    probs_again = jnp.exp(scores_of() - log_total)
    grad_probs = jnp.einsum(
        "tkgd,skd->kgts", grad_heads, value_heads, preferred_element_type=jnp.float32
    )
    inner = jnp.sum(probs_again * grad_probs, axis=-1, keepdims=True)
    grad_scores = (probs_again * (grad_probs - inner)).astype(jnp.bfloat16)
    grad_query_rows = (
        jnp.einsum("kgts,skd->tkgd", grad_scores, key_heads, preferred_element_type=jnp.float32)
        * qk_scale
    )
    grad_query_rows = grad_query_rows.reshape(local_rows, HEADS * HEAD).astype(jnp.bfloat16)
    grad_keys_all = (
        jnp.einsum("kgts,tkgd->skd", grad_scores, query_heads, preferred_element_type=jnp.float32)
        * qk_scale
    )
    grad_values_all = jnp.einsum(
        "kgts,tkgd->skd",
        probs_again.astype(jnp.bfloat16),
        grad_heads,
        preferred_element_type=jnp.float32,
    )
    key_sum, value_sum = tuple(
        (
            part.astype(jnp.float32)
            for part in in_one_piece(
                (
                    grad_keys_all.reshape(group_len, KV_HEADS * HEAD).astype(jnp.bfloat16),
                    grad_values_all.reshape(group_len, KV_HEADS * HEAD).astype(jnp.bfloat16),
                ),
                "fsdp",
                0,
                1,
            )
        )
    )
    grad_key_rows = key_sum.astype(jnp.bfloat16)
    grad_value_rows = value_sum.astype(jnp.bfloat16)
    query_back, key_back, value_back = (attn_in[1], attn_in[2], attn_in[3])
    grad_normed_one = (
        dot_rows(grad_query_rows, query_back)
        + dot_rows(grad_key_rows, key_back)
        + dot_rows(grad_value_rows, value_back)
    )
    grad_query = dot_cols(normed_one, grad_query_rows)
    grad_key = dot_cols(normed_one, grad_key_rows)
    grad_value = dot_cols(normed_one, grad_value_rows)
    grad_norm_one, grad_gain_attn = norm_back(grad_normed_one, unit_one, factor_one, gain_one)
    grad_input = (grad_hidden + grad_norm_one).astype(jnp.bfloat16)
    attn_owned = tuple(
        (
            part.astype(jnp.float32)
            for part in sent_together(
                (
                    grad_gain_attn.astype(jnp.bfloat16),
                    grad_query.astype(jnp.bfloat16),
                    grad_key.astype(jnp.bfloat16),
                    grad_value.astype(jnp.bfloat16),
                    grad_out.astype(jnp.bfloat16),
                ),
                "fsdp",
                0,
                1,
            )
        )
    )
    summed = (
        lax.psum(attn_owned[0].astype(jnp.bfloat16), "rep").astype(jnp.float32),
        lax.psum(attn_owned[1].astype(jnp.bfloat16), "rep").astype(jnp.float32),
        lax.psum(attn_owned[2].astype(jnp.bfloat16), "rep").astype(jnp.float32),
        lax.psum(attn_owned[3].astype(jnp.bfloat16), "rep").astype(jnp.float32),
        lax.psum(attn_owned[4].astype(jnp.bfloat16), "rep").astype(jnp.float32),
        lax.psum(ffn_owned[0].astype(jnp.bfloat16), "rep").astype(jnp.float32),
        lax.psum(ffn_owned[1].astype(jnp.bfloat16), "rep").astype(jnp.float32),
        lax.psum(ffn_owned[2].astype(jnp.bfloat16), "rep").astype(jnp.float32),
        lax.psum(ffn_owned[4].astype(jnp.bfloat16), "rep").astype(jnp.float32),
        lax.psum(ffn_owned[3].astype(jnp.bfloat16), "rep").astype(jnp.float32),
        lax.psum(ffn_owned[5].astype(jnp.bfloat16), "rep").astype(jnp.float32),
    )
    return (
        result.astype(jnp.bfloat16),
        grad_input,
        summed[0],
        summed[1],
        summed[2],
        summed[3],
        summed[4],
        summed[5],
        summed[6],
        summed[7],
        summed[8],
        summed[9],
        summed[10],
    )


def solution(mesh):
    return jax.shard_map(
        shards,
        mesh=mesh,
        in_specs=(
            P(("rep", "fsdp"), None),
            P("rep"),
            P(("rep", "fsdp"), None),
            P("fsdp"),
            P("fsdp", None),
            P("fsdp", None),
            P("fsdp", None),
            P("fsdp", None),
            P("fsdp"),
            P("fsdp", None),
            P("fsdp", None),
            P("fsdp", None),
            P("fsdp", None, None),
            P(None, "fsdp", None),
            P(("rep", "fsdp"), None),
        ),
        out_specs=(
            P(("rep", "fsdp"), None),
            P(("rep", "fsdp"), None),
            P("fsdp"),
            P("fsdp", None),
            P("fsdp", None),
            P("fsdp", None),
            P("fsdp", None),
            P("fsdp"),
            P("fsdp", None),
            P("fsdp", None),
            P("fsdp", None),
            P("fsdp", None, None),
            P(None, "fsdp", None),
        ),
        check_vma=False,
    )
```

profile of v0, /device:TPU:1, one launch (start us, length us, event | category | flops | bytes accessed | tf_op | source)
XLA Modules:
  0.0 1894.8 jit_solution(13531483751671472540)
XLA Ops:
  10.9 116.5 %all-gather.11.cloned.1.call-done = bf16[1536,2561]{1,0:T(8,128)(2,1)} async-done(((bf16[192,2561]{1,0:T(8,128)(2,1)}), bf16[1536,2561]{1,0:T(8,128)(2,1)}) %all-gather.11.cloned.1.call-update) | async-done | bytes 7867408 | tf_op jit(solution)/shard_map/all_gather | solution.py:20
  141.0 5.3 copy.155
  148.5 16.4 all-reduce
  164.9 27.8 %all-gather.1 = bf16[8,192,8]{1,2,0:T(8,128)(2,1)S(1)} all-gather(bf16[1,192,8]{1,2,0:T(8,128)(2,1)S(1)} %bitcast.143), channel_id=1, replica_groups=mesh['rep'=32,'fsdp'=8] {'fsdp'}, dimensions={0}, use_global_device_ids=true | all-gather | bytes 27648 | tf_op jit(solution)/shard_map/all_gather | solution.py:174
  210.6 64.4 %all-gather.15.cloned.1.call-done = bf16[1536,1536]{1,0:T(8,128)(2,1)} async-done(((bf16[192,1536]{1,0:T(8,128)(2,1)}), bf16[1536,1536]{1,0:T(8,128)(2,1)}) %all-gather.15.cloned.1.call-update) | async-done | bytes 4718608 | tf_op jit(solution)/shard_map/all_gather | solution.py:170
  281.7 88.5 %all-gather.19.cloned.1.call-done = bf16[1536,2048]{1,0:T(8,128)(2,1)} async-done(((bf16[192,2048]{1,0:T(8,128)(2,1)}), bf16[1536,2048]{1,0:T(8,128)(2,1)}) %all-gather.19.cloned.1.call-update) | async-done | bytes 6291472 | tf_op jit(solution)/shard_map/all_gather | solution.py:175
  370.2 4.7 fusion.108
  375.0 177.1 %all-gather.25.cloned.1.call-done = bf16[7864320]{0:T(1024)(128)(2,1)} async-done(((bf16[983040]{0:T(1024)(128)(2,1)}), bf16[7864320]{0:T(1024)(128)(2,1)}) %all-gather.25.cloned.1.call-update) | async-done | bytes 15728656 | tf_op jit(solution)/shard_map/all_gather | solution.py:44
  552.1 20.6 %reshape.239 = bf16[8,983040]{1,0:T(8,128)(2,1)} reshape(bf16[7864320]{0:T(1024)(128)(2,1)} %all-gather.25.cloned.1.call-done) | data formatting | bytes 31457280 | tf_op jit(solution)/shard_map/all_gather | solution.py:44
  572.6 10.8 slice.46
  586.6 13.2 copy.156
  602.0 219.1 %all-gather.17.cloned.1.call-done = bf16[1536,8,1024]{2,0,1:T(8,128)(2,1)} async-done(((bf16[192,8,1024]{2,0,1:T(8,128)(2,1)}), bf16[1536,8,1024]{2,0,1:T(8,128)(2,1)}) %all-gather.17.cloned.1.call-update) | async-done | bytes 25165840 | tf_op jit(solution)/shard_map/all_gather | solution.py:176
  821.1 10.0 fusion.78
  831.1 10.4 fusion.35
  853.2 13.4 convolution_bitcast_fusion.1
  866.7 5.2 convolution_add_fusion.5
  873.2 5.0 convolution_convert_fusion.4
  913.4 56.0 %reduce-scatter.7.cloned.1.call-done = bf16[128,1024]{1,0:T(8,128)(2,1)} async-done(((bf16[1024,1024]{1,0:T(8,128)(2,1)}), bf16[128,1024]{1,0:T(8,128)(2,1)}) %reduce-scatter.7.cloned.1.call-update) | async-done | bytes 262160
  977.6 63.8 %concatenate.35 = bf16[1536,4097]{0,1:T(8,128)(2,1)} concatenate(bf16[1536,1]{0,1:T(2,128)(2,1)S(1)} %convert_element_type.236, bf16[1536,1536]{0,1:T(8,128)(2,1)} %convolution_convert_fusion, bf16[1536,512]{0,1:T(8,128)(2,1)S(1)} %convolution_convert_fusion.3, bf16[1536,512]{0,1:T(8,128)(2,1)} %convolution_convert_fusion.2, bf16[1536,1536]{0,1:T(8,128)(2,1)} %convolution_convert_fusion.1), dimensions={1} | concatenate | bytes 25171968 | tf_op jit(solution)/shard_map/concatenate | solution.py:72
  1041.4 16.6 copy.206
  1058.7 75.8 %all-gather.23.cloned.1.call-done = bf16[1024,6656]{1,0:T(8,128)(2,1)} async-done(((bf16[128,6656]{1,0:T(8,128)(2,1)}), bf16[1024,6656]{1,0:T(8,128)(2,1)}) %all-gather.23.cloned.1.call-update) | async-done | bytes 13631504 | tf_op jit(solution)/shard_map/all_gather | solution.py:20
  1134.4 7.9 split.74
  1142.3 11.9 copy.203
  1159.1 5.1 fusion.17
  1164.2 133.3 %reduce-scatter.9.cloned.1.call-done = bf16[192,4097]{1,0:T(8,128)(2,1)} async-done(((bf16[1536,4097]{1,0:T(8,128)(2,1)}), bf16[192,4097]{1,0:T(8,128)(2,1)}) %reduce-scatter.9.cloned.1.call-update) | async-done | bytes 1573264
  1304.5 279.1 %all-gather.21.cloned.1.call-done = bf16[1024,11784]{0,1:T(8,128)(2,1)} async-done(((bf16[128,11784]{0,1:T(8,128)(2,1)}), bf16[1024,11784]{0,1:T(8,128)(2,1)}) %all-gather.21.cloned.1.call-update) | async-done | bytes 24133648 | tf_op jit(solution)/shard_map/all_gather | solution.py:20
  1587.5 13.8 split.73
  1601.3 13.2 convolution_convert_fusion.5
  1614.5 4.7 fusion.23
  1624.1 6.5 fusion.26
  1635.2 56.7 %all-reduce.1 = (bf16[192]{0:T(256)(128)(2,1)S(1)}, bf16[192]{0:T(256)(128)(2,1)S(1)}, bf16[192,8]{0,1:T(8,128)(2,1)S(1)}) all-reduce(bf16[192]{0:T(256)(128)(2,1)S(1)} %slice_reduce_fusion, bf16[192]{0:T(256)(128)(2,1)S(1)} %reduce_sum.129, bf16[192,8]{0,1:T(8,128)(2,1)S(1)} %convolution_convert_fusion.6), channel_id=1, replica_groups=mesh['rep'=32,'fsdp'=8] {'rep'}, use_global_device_ids=true, to_apply=%region_14.15 | all-reduce | flops 1920 | bytes 7680 | tf_op jit(solution)/shard_map/psum | solution.py:332
  1693.6 177.9 %all-reduce.5.cloned.1.call-done = (bf16[192,1536]{0,1:T(8,128)(2,1)}, bf16[192,512]{0,1:T(8,128)(2,1)}, bf16[192,512]{0,1:T(8,128)(2,1)}, bf16[192,1536]{0,1:T(...) async-done(((bf16[192,1536]{0,1:T(8,128)(2,1)}, bf16[192,512]{0,1:T(8,128)(2,1)}, ...) | async-done | bytes 7471120 | tf_op jit(solution)/shard_map/psum | solution.py:333
  (252 shorter events, 148.4 us)
Async XLA Ops:
  7.2 120.2 %all-gather.11.cloned.1.call-start = ((), (), s32[]{:S(2)}) async-start(), calls=%async_computation.3 | async-start | bytes 9289728 | tf_op jit(solution)/shard_map/all_gather | solution.py:20
  10.7 187.1 %all-gather.13.cloned.1.call-start = ((), (), s32[]{:S(2)}) async-start(), calls=%async_computation.4 | async-start | bytes 2359296 | tf_op jit(solution)/shard_map/all_gather | solution.py:33
  10.9 182.5 %copy-start.48 = (f32[128]{0:T(128)}, f32[128]{0:T(128)S(1)}, u32[]{:S(2)}) copy-start(f32[128]{0:T(128)S(1)} %add_rsqrt_fusion.1) | copy-start | bytes 1540
  134.1 140.9 %all-gather.15.cloned.1.call-start = ((), (), s32[]{:S(2)}) async-start(), calls=%async_computation.5 | async-start | bytes 5308416 | tf_op jit(solution)/shard_map/all_gather | solution.py:170
  134.9 235.3 %all-gather.19.cloned.1.call-start = ((), (), s32[]{:S(2)}) async-start(), calls=%async_computation.7 | async-start | bytes 7077888 | tf_op jit(solution)/shard_map/all_gather | solution.py:175
  135.4 416.6 %all-gather.25.cloned.1.call-start = ((), (), s32[]{:S(2)}) async-start(), calls=%async_computation.10 | async-start | bytes 17694720 | tf_op jit(solution)/shard_map/all_gather | solution.py:44
  141.0 680.1 %all-gather.17.cloned.1.call-start = ((), (), s32[]{:S(2)}) async-start(), calls=%async_computation.6 | async-start | bytes 28311552 | tf_op jit(solution)/shard_map/all_gather | solution.py:176
  146.3 18.6 copy-start.52
  146.3 46.6 %copy-start.45 = (s32[1024]{0:T(1024)S(1)}, s32[1024]{0:T(1024)}, u32[]{:S(2)}) copy-start(s32[1024]{0:T(1024)} %param.16) | copy-start | bytes 12292
  146.3 46.6 %copy-start.53 = (s32[128,6]{0,1:T(8,128)S(1)}, s32[128,6]{0,1:T(8,128)}, u32[]{:S(2)}) copy-start(s32[128,6]{0,1:T(8,128)} %param.17) | copy-start | bytes 9220
  146.4 823.0 %reduce-scatter.7.cloned.1.call-start = ((), (), s32[]{:S(2)}) async-start(), calls=%async_computation.11 | async-start | bytes 2359296
  164.9 113.4 %copy-start.40 = (f32[1536]{0:T(1024)}, f32[1536]{0:T(1024)S(1)}, u32[]{:S(2)}) copy-start(f32[1536]{0:T(1024)S(1)} %convert_element_type.213) | copy-start | bytes 18436
  192.9 86.7 %copy-start.38 = (bf16[1536,8]{0,1:T(8,128)(2,1)}, bf16[1536,8]{0,1:T(8,128)(2,1)S(1)}, u32[]{:S(2)}) copy-start(bf16[1536,8]{0,1:T(8,128)(2,1)S(1)} %reshape.244) | copy-start | bytes 73732
  210.6 67.7 %copy-start.23 = (bf16[4,128,3,128]{3,1,2,0:T(8,128)(2,1)}, bf16[4,128,3,128]{3,1,2,0:T(8,128)(2,1)S(1)}, u32[]{:S(2)}) copy-start(bf16[4,128,3,128]{3,1,2,0:T(8,128)(2,1)S(1)} %fusion.45) | copy-start | bytes 1179652
  278.3 96.7 %copy-start.50 = (f32[128]{0:T(128)}, f32[128]{0:T(128)S(1)}, u32[]{:S(2)}) copy-start(f32[128]{0:T(128)S(1)} %add_rsqrt_fusion) | copy-start | bytes 1540
  279.3 95.7 %copy-start.8 = (bf16[128,1536]{1,0:T(8,128)(2,1)}, bf16[128,1536]{1,0:T(8,128)(2,1)S(1)}, u32[]{:S(2)}) copy-start(bf16[128,1536]{1,0:T(8,128)(2,1)S(1)} %multiply_convert_fusion.1) | copy-start | bytes 1179652
  572.6 10.8 slice-start.2
  586.6 13.2 copy-start.10
  586.6 13.2 copy-start.27
  586.6 13.2 copy-start.29
  599.7 221.3 %copy-start.9 = (bf16[128,1536]{1,0:T(8,128)(2,1)S(1)}, bf16[128,1536]{1,0:T(8,128)(2,1)}, u32[]{:S(2)}) copy-start(bf16[128,1536]{1,0:T(8,128)(2,1)} %copy-done.8) | copy-start | bytes 1179652
  601.7 229.4 %copy-start.30 = (bf16[128,1024]{1,0:T(8,128)(2,1)}, bf16[128,1024]{1,0:T(8,128)(2,1)S(1)}, u32[]{:S(2)}) copy-start(bf16[128,1024]{1,0:T(8,128)(2,1)S(1)} %get-tuple-element.106) | copy-start | bytes 786436
  831.1 10.5 copy-start.3
  831.1 10.4 copy-start.46
  831.1 10.4 copy-start.54
  841.5 11.1 copy-start.42
  873.2 11.2 slice-start
  891.8 242.6 %all-gather.23.cloned.1.call-start = ((), (), s32[]{:S(2)}) async-start(), calls=%async_computation.9 | async-start | bytes 15335424 | tf_op jit(solution)/shard_map/all_gather | solution.py:20
  901.6 395.9 %reduce-scatter.9.cloned.1.call-start = ((), (), s32[]{:S(2)}) async-start(), calls=%async_computation.12 | async-start | bytes 14598144
  1058.0 525.6 %all-gather.21.cloned.1.call-start = ((), (), s32[]{:S(2)}) async-start(), calls=%async_computation.8 | async-start | bytes 27150336 | tf_op jit(solution)/shard_map/all_gather | solution.py:20
  1058.6 812.9 %all-reduce.5.cloned.1.call-start = ((), (), s32[]{:S(2)}) async-start(), calls=%async_computation.13 | async-start | bytes 15990784 | tf_op jit(solution)/shard_map/psum | solution.py:333
  1620.6 11.4 all-to-all-start
  (43 other events, 179.6 us)
Sparse Core Ops, SparseCore 0:
  11.2 116.1 all-gather.10
  134.2 57.2 all-gather.12
  194.2 80.7 all-gather.14
  277.5 92.6 all-gather.18
  372.7 179.3 all-gather.24
  555.0 265.9 all-gather.16
  891.9 77.3 reduce-scatter.6
  972.3 162.0 all-gather.22
  1139.3 158.1 reduce-scatter.8
  1299.8 283.7 all-gather.20
  1619.4 252.0 all-reduce.4
where the time goes:
time: 1910 us; the launch traced here: 1890 us
  waiting for transfers between devices  1390 us (73%)
  local copies, waits for them, and re-layouts  232 us (12%)
  matrix products  130 us (7%)
  blocking collectives  101 us (5%)
  other arithmetic  23.6 us (1%)
    all_gather x3, waiting for transfers between devices, side_by_side(): whole = lax.all_gather(both, axis, axis=dim, tiled=True)  471 us
    all_gather x1, waiting for transfers between devices, shards(): lax.all_gather(w_expert_in, 'fsdp', axis=0, tiled=True)  219 us
    unnamed x13, waiting for transfers between devices  191 us
    psum x1, waiting for transfers between devices, shards(): lax.psum(attn_owned[1].astype(jnp.bfloat16), 'rep').astype(jnp.float32)  178 us
    all_gather x1, waiting for transfers between devices, gather_packed(): lines, at, gathered = (lax.all_gather(flat, axis), 0, [])  177 us
    all_gather x1, waiting for transfers between devices, shards(): lax.all_gather(w_shared_in, 'fsdp', axis=0, tiled=True)  88.5 us
    all_gather x1, waiting for transfers between devices, shards(): out_full = lax.all_gather(w_out, 'fsdp', axis=0, tiled=True)  64.4 us
    concatenate x1, local copies, waits for them, and re-layouts, sent_together(): both = jnp.concatenate(columns, axis=along)  63.8 us
  transfers between devices with their start and end apart: 12, of which 10 were waited for; matrix products, arithmetic and copies ran while one was open for 13% of the time, Pallas kernels for 0%

commit v1 on v0

--- a/solution.py
+++ b/solution.py
@@ -167,7 +167,9 @@
     probs = (expo / total).astype(jnp.bfloat16)
     attended = jnp.einsum("kgts,skd->tkgd", probs, value_heads, preferred_element_type=jnp.float32)
     attended = attended.reshape(local_rows, HEADS * HEAD).astype(jnp.bfloat16)
-    out_full = lax.all_gather(w_out, "fsdp", axis=0, tiled=True)
+    out_full = jnp.concatenate(
+        lax.all_to_all(jnp.stack([w_out] * lax.axis_size("fsdp")), "fsdp", 0, 0), axis=0
+    )
     hidden = inputs + jnp.dot(attended, out_full, preferred_element_type=jnp.float32)
     ffn_in = (
         lax.all_gather(gain_ffn, "fsdp", axis=0, tiled=True),

time: 1910 us -> 1870 us (0.979)
  waiting for transfers between devices: 1390 us -> 1280 us
  blocking collectives: 101 us -> 163 us
    all_gather x1 -> x0, waiting for transfers between devices: 64.4 us -> none  [shards(): out_full = lax.all_gather(w_out, 'fsdp', axis=0, tiled=True)]
    unnamed x1, blocking collectives: 16.4 us -> 78.5 us
    all_gather x1, waiting for transfers between devices: 88.5 us -> 42.7 us  [shards(): lax.all_gather(w_shared_in, 'fsdp', axis=0, tiled=True)]
    unnamed x142 -> x144, local copies, waits for them, and re-layouts: 51.8 us -> 52.3 us
    unnamed x13 -> x12, waiting for transfers between devices: 191 us -> 191 us
  transfers between devices with their start and end apart: 12 -> 12, of which waited for: 10 -> 9; matrix products, arithmetic and copies ran while one was open for 13% -> 13% of each run, Pallas kernels for 0% -> 0%
where the time goes in v1:
time: 1870 us; the launch traced here: 1850 us
  waiting for transfers between devices  1280 us (68%)
  local copies, waits for them, and re-layouts  235 us (13%)
  blocking collectives  163 us (9%)
  matrix products  130 us (7%)
  other arithmetic  23.5 us (1%)
    all_gather x3, waiting for transfers between devices, side_by_side(): whole = lax.all_gather(both, axis, axis=dim, tiled=True)  471 us
    all_gather x1, waiting for transfers between devices, shards(): lax.all_gather(w_expert_in, 'fsdp', axis=0, tiled=True)  219 us
    unnamed x12, waiting for transfers between devices  191 us
    psum x1, waiting for transfers between devices, shards(): lax.psum(attn_owned[1].astype(jnp.bfloat16), 'rep').astype(jnp.float32)  178 us
    all_gather x1, waiting for transfers between devices, gather_packed(): lines, at, gathered = (lax.all_gather(flat, axis), 0, [])  177 us
    unnamed x1, blocking collectives  78.5 us
    concatenate x1, local copies, waits for them, and re-layouts, sent_together(): both = jnp.concatenate(columns, axis=along)  63.7 us
    psum x1, blocking collectives, shards(): lax.psum(attn_owned[0].astype(jnp.bfloat16), 'rep').astype(jnp.float32)  56.9 us
  transfers between devices with their start and end apart: 12, of which 9 were waited for; matrix products, arithmetic and copies ran while one was open for 13% of the time, Pallas kernels for 0%

profile of v1, /device:TPU:1, one launch (start us, length us, event | category | flops | bytes accessed | tf_op | source)
XLA Modules:
  0.0 1854.5 jit_solution(3741494863714712255)
XLA Ops:
  10.9 116.5 %all-gather.10.cloned.1.call-done = bf16[1536,2561]{1,0:T(8,128)(2,1)} async-done(((bf16[192,2561]{1,0:T(8,128)(2,1)}), bf16[1536,2561]{1,0:T(8,128)(2,1)}) %all-gather.10.cloned.1.call-update) | async-done | bytes 7867408 | tf_op jit(solution)/shard_map/all_gather | solution.py:20
  140.5 5.3 copy.155
  149.4 4.8 all-to-all-start
  155.8 78.5 %all-reduce = bf16[1536]{0:T(1024)(128)(2,1)S(1)} all-reduce(bf16[1536]{0:T(1024)(128)(2,1)S(1)} %dynamic-update-slice), channel_id=1, replica_groups=mesh['rep'=32,'fsdp'=8] {'fsdp'}, use_global_device_ids=true, to_apply=%add | all-reduce | flops 1536 | bytes 6144
  234.3 27.7 %all-gather.1 = bf16[8,192,8]{1,2,0:T(8,128)(2,1)S(1)} all-gather(bf16[1,192,8]{1,2,0:T(8,128)(2,1)S(1)} %bitcast.144), channel_id=1, replica_groups=mesh['rep'=32,'fsdp'=8] {'fsdp'}, dimensions={0}, use_global_device_ids=true | all-gather | bytes 27648 | tf_op jit(solution)/shard_map/all_gather | solution.py:176
  286.7 42.7 %all-gather.16.cloned.1.call-done = bf16[1536,2048]{1,0:T(8,128)(2,1)} async-done(((bf16[192,2048]{1,0:T(8,128)(2,1)}), bf16[1536,2048]{1,0:T(8,128)(2,1)}) %all-gather.16.cloned.1.call-update) | async-done | bytes 6291472 | tf_op jit(solution)/shard_map/all_gather | solution.py:177
  329.4 4.7 fusion.108
  334.1 177.1 %all-gather.22.cloned.1.call-done = bf16[7864320]{0:T(1024)(128)(2,1)} async-done(((bf16[983040]{0:T(1024)(128)(2,1)}), bf16[7864320]{0:T(1024)(128)(2,1)}) %all-gather.22.cloned.1.call-update) | async-done | bytes 15728656 | tf_op jit(solution)/shard_map/all_gather | solution.py:44
  511.2 20.6 %reshape.246 = bf16[8,983040]{1,0:T(8,128)(2,1)} reshape(bf16[7864320]{0:T(1024)(128)(2,1)} %all-gather.22.cloned.1.call-done) | data formatting | bytes 31457280 | tf_op jit(solution)/shard_map/all_gather | solution.py:44
  531.8 10.8 slice.46
  545.7 13.2 copy.156
  561.2 219.1 %all-gather.14.cloned.1.call-done = bf16[1536,8,1024]{2,0,1:T(8,128)(2,1)} async-done(((bf16[192,8,1024]{2,0,1:T(8,128)(2,1)}), bf16[1536,8,1024]{2,0,1:T(8,128)(2,1)}) %all-gather.14.cloned.1.call-update) | async-done | bytes 25165840 | tf_op jit(solution)/shard_map/all_gather | solution.py:178
  780.2 10.0 fusion.78
  790.3 10.4 fusion.35
  812.4 13.4 convolution_bitcast_fusion.1
  825.8 5.2 convolution_add_fusion.5
  832.4 5.0 convolution_convert_fusion.4
  872.6 56.0 %reduce-scatter.7.cloned.1.call-done = bf16[128,1024]{1,0:T(8,128)(2,1)} async-done(((bf16[1024,1024]{1,0:T(8,128)(2,1)}), bf16[128,1024]{1,0:T(8,128)(2,1)}) %reduce-scatter.7.cloned.1.call-update) | async-done | bytes 262160
  936.8 63.7 %concatenate.35 = bf16[1536,4097]{0,1:T(8,128)(2,1)} concatenate(bf16[1536,1]{0,1:T(2,128)(2,1)S(1)} %convert_element_type.238, bf16[1536,1536]{0,1:T(8,128)(2,1)} %convolution_convert_fusion, bf16[1536,512]{0,1:T(8,128)(2,1)S(1)} %convolution_convert_fusion.3, bf16[1536,512]{0,1:T(8,128)(2,1)} %convolution_convert_fusion.2, bf16[1536,1536]{0,1:T(8,128)(2,1)} %convolution_convert_fusion.1), dimensions={1} | concatenate | bytes 25171968 | tf_op jit(solution)/shard_map/concatenate | solution.py:72
  1000.6 16.6 copy.206
  1018.0 75.6 %all-gather.20.cloned.1.call-done = bf16[1024,6656]{1,0:T(8,128)(2,1)} async-done(((bf16[128,6656]{1,0:T(8,128)(2,1)}), bf16[1024,6656]{1,0:T(8,128)(2,1)}) %all-gather.20.cloned.1.call-update) | async-done | bytes 13631504 | tf_op jit(solution)/shard_map/all_gather | solution.py:20
  1093.5 7.9 split.74
  1101.4 11.9 copy.203
  1118.2 5.1 fusion.17
  1123.3 133.3 %reduce-scatter.9.cloned.1.call-done = bf16[192,4097]{1,0:T(8,128)(2,1)} async-done(((bf16[1536,4097]{1,0:T(8,128)(2,1)}), bf16[192,4097]{1,0:T(8,128)(2,1)}) %reduce-scatter.9.cloned.1.call-update) | async-done | bytes 1573264
  1263.6 279.2 %all-gather.18.cloned.1.call-done = bf16[1024,11784]{0,1:T(8,128)(2,1)} async-done(((bf16[128,11784]{0,1:T(8,128)(2,1)}), bf16[1024,11784]{0,1:T(8,128)(2,1)}) %all-gather.18.cloned.1.call-update) | async-done | bytes 24133648 | tf_op jit(solution)/shard_map/all_gather | solution.py:20
  1546.7 13.8 split.73
  1560.6 13.2 convolution_convert_fusion.5
  1573.8 4.7 fusion.23
  1583.3 6.5 fusion.26
  1594.5 56.9 %all-reduce.1 = (bf16[192]{0:T(256)(128)(2,1)S(1)}, bf16[192]{0:T(256)(128)(2,1)S(1)}, bf16[192,8]{0,1:T(8,128)(2,1)S(1)}) all-reduce(bf16[192]{0:T(256)(128)(2,1)S(1)} %slice_reduce_fusion, bf16[192]{0:T(256)(128)(2,1)S(1)} %reduce_sum.129, bf16[192,8]{0,1:T(8,128)(2,1)S(1)} %convolution_convert_fusion.6), channel_id=1, replica_groups=mesh['rep'=32,'fsdp'=8] {'rep'}, use_global_device_ids=true, to_apply=%region_14.15 | all-reduce | flops 1920 | bytes 7680 | tf_op jit(solution)/shard_map/psum | solution.py:334
  1653.1 177.9 %all-reduce.5.cloned.1.call-done = (bf16[192,1536]{0,1:T(8,128)(2,1)}, bf16[192,512]{0,1:T(8,128)(2,1)}, bf16[192,512]{0,1:T(8,128)(2,1)}, bf16[192,1536]{0,1:T(...) async-done(((bf16[192,1536]{0,1:T(8,128)(2,1)}, bf16[192,512]{0,1:T(8,128)(2,1)}, ...) | async-done | bytes 7471120 | tf_op jit(solution)/shard_map/psum | solution.py:335
  (254 shorter events, 151.2 us)
Async XLA Ops:
  7.2 120.2 %all-gather.10.cloned.1.call-start = ((), (), s32[]{:S(2)}) async-start(), calls=%async_computation.4 | async-start | bytes 9289728 | tf_op jit(solution)/shard_map/all_gather | solution.py:20
  10.7 256.4 %all-gather.12.cloned.1.call-start = ((), (), s32[]{:S(2)}) async-start(), calls=%async_computation.5 | async-start | bytes 2359296 | tf_op jit(solution)/shard_map/all_gather | solution.py:33
  10.9 251.7 %copy-start.49 = (f32[128]{0:T(128)}, f32[128]{0:T(128)S(1)}, u32[]{:S(2)}) copy-start(f32[128]{0:T(128)S(1)} %add_rsqrt_fusion.1) | copy-start | bytes 1540
  134.1 195.2 %all-gather.16.cloned.1.call-start = ((), (), s32[]{:S(2)}) async-start(), calls=%async_computation.7 | async-start | bytes 7077888 | tf_op jit(solution)/shard_map/all_gather | solution.py:177
  134.9 376.4 %all-gather.22.cloned.1.call-start = ((), (), s32[]{:S(2)}) async-start(), calls=%async_computation.10 | async-start | bytes 17694720 | tf_op jit(solution)/shard_map/all_gather | solution.py:44
  140.4 639.8 %all-gather.14.cloned.1.call-start = ((), (), s32[]{:S(2)}) async-start(), calls=%async_computation.6 | async-start | bytes 28311552 | tf_op jit(solution)/shard_map/all_gather | solution.py:178
  149.4 84.9 %copy-start.53 = (bf16[192,8]{0,1:T(8,128)(2,1)S(1)}, bf16[192,8]{0,1:T(8,128)(2,1)}, u32[]{:S(2)}) copy-start(bf16[192,8]{0,1:T(8,128)(2,1)} %param.24) | copy-start | bytes 9220
  149.4 112.7 %copy-start.46 = (s32[1024]{0:T(1024)S(1)}, s32[1024]{0:T(1024)}, u32[]{:S(2)}) copy-start(s32[1024]{0:T(1024)} %param.16) | copy-start | bytes 12292
  149.4 112.8 %copy-start.54 = (s32[128,6]{0,1:T(8,128)S(1)}, s32[128,6]{0,1:T(8,128)}, u32[]{:S(2)}) copy-start(s32[128,6]{0,1:T(8,128)} %param.17) | copy-start | bytes 9220
  149.4 130.5 %all-to-all-start = ((bf16[8,192,1536]{2,1,0:T(8,128)(2,1)}), bf16[8,192,1536]{2,1,0:T(8,128)(2,1)}, u32[]{:S(2)}, u32[]{:S(2)}) async-start(bf16[8,192,1536]{2,1,0:T(8,128)(2,1)} %stack.2), calls=%async_computation | async-start | bytes 9437184 | tf_op jit(solution)/shard_map/all_to_all | solution.py:171
  154.2 774.4 %reduce-scatter.7.cloned.1.call-start = ((), (), s32[]{:S(2)}) async-start(), calls=%async_computation.11 | async-start | bytes 2359296
  234.3 49.0 %copy-start.41 = (f32[1536]{0:T(1024)}, f32[1536]{0:T(1024)S(1)}, u32[]{:S(2)}) copy-start(f32[1536]{0:T(1024)S(1)} %convert_element_type.215) | copy-start | bytes 18436
  262.1 22.4 %copy-start.39 = (bf16[1536,8]{0,1:T(8,128)(2,1)}, bf16[1536,8]{0,1:T(8,128)(2,1)S(1)}, u32[]{:S(2)}) copy-start(bf16[1536,8]{0,1:T(8,128)(2,1)S(1)} %reshape.251) | copy-start | bytes 73732
  283.3 50.8 %copy-start.51 = (f32[128]{0:T(128)}, f32[128]{0:T(128)S(1)}, u32[]{:S(2)}) copy-start(f32[128]{0:T(128)S(1)} %add_rsqrt_fusion) | copy-start | bytes 1540
  284.3 49.8 %copy-start.8 = (bf16[128,1536]{1,0:T(8,128)(2,1)}, bf16[128,1536]{1,0:T(8,128)(2,1)S(1)}, u32[]{:S(2)}) copy-start(bf16[128,1536]{1,0:T(8,128)(2,1)S(1)} %multiply_convert_fusion.1) | copy-start | bytes 1179652
  531.8 10.8 slice-start.2
  545.7 13.2 copy-start.10
  545.7 13.2 copy-start.27
  545.7 13.2 copy-start.29
  558.9 221.3 %copy-start.9 = (bf16[128,1536]{1,0:T(8,128)(2,1)S(1)}, bf16[128,1536]{1,0:T(8,128)(2,1)}, u32[]{:S(2)}) copy-start(bf16[128,1536]{1,0:T(8,128)(2,1)} %copy-done.8) | copy-start | bytes 1179652
  560.8 229.4 %copy-start.30 = (bf16[128,1024]{1,0:T(8,128)(2,1)}, bf16[128,1024]{1,0:T(8,128)(2,1)S(1)}, u32[]{:S(2)}) copy-start(bf16[128,1024]{1,0:T(8,128)(2,1)S(1)} %get-tuple-element.106) | copy-start | bytes 786436
  790.3 10.5 copy-start.3
  790.3 10.4 copy-start.47
  790.3 10.4 copy-start.55
  800.7 11.1 copy-start.43
  832.4 11.2 slice-start
  851.0 242.6 %all-gather.20.cloned.1.call-start = ((), (), s32[]{:S(2)}) async-start(), calls=%async_computation.9 | async-start | bytes 15335424 | tf_op jit(solution)/shard_map/all_gather | solution.py:20
  860.8 395.9 %reduce-scatter.9.cloned.1.call-start = ((), (), s32[]{:S(2)}) async-start(), calls=%async_computation.12 | async-start | bytes 14598144
  1017.2 525.7 %all-gather.18.cloned.1.call-start = ((), (), s32[]{:S(2)}) async-start(), calls=%async_computation.8 | async-start | bytes 27150336 | tf_op jit(solution)/shard_map/all_gather | solution.py:20
  1017.9 813.0 %all-reduce.5.cloned.1.call-start = ((), (), s32[]{:S(2)}) async-start(), calls=%async_computation.13 | async-start | bytes 15990784 | tf_op jit(solution)/shard_map/psum | solution.py:335
  1579.9 11.4 all-to-all-start.1
  1831.0 8.5 copy-start.33
  (44 other events, 185.1 us)
Sparse Core Ops, SparseCore 0:
  11.2 116.1 all-gather.9
  134.3 98.3 all-gather.11
  235.3 94.0 all-gather.15
  331.8 179.3 all-gather.21
  514.2 265.9 all-gather.13
  851.1 77.3 reduce-scatter.6
  931.5 161.9 all-gather.19
  1098.4 158.2 reduce-scatter.8
  1259.1 283.7 all-gather.17
  1578.7 252.2 all-reduce.4
